TPU v7x, 128 devices: a whole 4x4x4 slice. The times are simulated.
128 devices in a mesh: role: 2 (over core), dev: 64 (over y, x, z).
Axes of the slice: x: 4, y: 4, z: 4, core: 2. Of those that a mesh axis runs over, the one named last changes fastest.
Arguments:
- queries: bfloat16 [2048, 32, 128], P('dev', 'role'), may hold values from -8 to 8
- keys_cache: bfloat16 [2048, 2, 192, 128], P('dev', 'role'), may hold values from -4 to 4
- values_cache: bfloat16 [2048, 2, 192, 128], P('dev', 'role'), may hold values from -4 to 4
- new_keys: bfloat16 [2048, 2, 128], P('dev', 'role'), may hold values from -4 to 4
- new_values: bfloat16 [2048, 2, 128], P('dev', 'role'), may hold values from -4 to 4
- lengths: int32 [2048], P('dev'), may hold values from 2 to 192, as said below
- norm_gain: float32 [4096], replicated, may hold values from 0.5 to 1.5
- expert_ids: int32 [2048, 8], P('dev'), may hold values from 0 to 127, all different within a row; in each aligned block of 16 rows (0 to 15, 16 to 31, ...) at most 2 rows name the same one
- route_weights: float32 [2048, 8], P('dev'), may hold values from 0.05 to 1
- gate_weight: bfloat16 [128, 4096, 768], P(('role', 'dev')), may hold values from -0.09375 to 0.09375
- up_weight: bfloat16 [128, 4096, 768], P(('role', 'dev')), may hold values from -0.09375 to 0.09375
- down_weight: bfloat16 [128, 768, 4096], P(('role', 'dev')), may hold values from -0.21875 to 0.21875
Outputs:
- mixed: bfloat16 [64, 2, 16, 4096], P('dev', 'role')
Inputs may be any that keep to these rules, and one draw needn't show every extreme that they name: `lengths`: request 0's cache is full. `expert_ids`: in each aligned block of 16 rows (the tokens that one device routes) no expert is named by more than 2 rows.
All inputs are finite; a program needn't handle non-finite values.
Results may differ from a plain program's by a relative error of at most 0.013.
Values may be sent and summed in bfloat16 or wider, within the bound.
A program may use at most 128 MiB of HBM per device.

v0:
```python
import jax
import jax.numpy as jnp
from jax import lax
from jax.sharding import PartitionSpec as P

HEAD = 128


def run_expert(rows, gate_weight, up_weight, down_weight):
    sources, slots, width = rows.shape
    flat = rows.reshape(sources * slots, width)
    gate = jnp.dot(flat, gate_weight[0], preferred_element_type=jnp.float32)
    up_part = jnp.dot(flat, up_weight[0], preferred_element_type=jnp.float32)
    hidden = (jax.nn.silu(gate) * up_part).astype(jnp.bfloat16)
    out = jnp.dot(hidden, down_weight[0], preferred_element_type=jnp.float32)
    return out.astype(jnp.bfloat16).reshape(sources, slots, width)


def per_device(
    queries,
    keys_cache,
    values_cache,
    new_keys,
    new_values,
    lengths,
    norm_gain,
    expert_ids,
    route_weights,
    gate_weight,
    up_weight,
    down_weight,
):
    scale = HEAD ** (-0.5)
    cached_keys = keys_cache[:, 0]
    cached_values = values_cache[:, 0]
    scores = (
        jnp.einsum("rgd,rld->rgl", queries, cached_keys, preferred_element_type=jnp.float32) * scale
    )
    valid = (
        jnp.arange(cached_keys.shape[1], dtype=jnp.int32)[None, None, :] < lengths[:, None, None]
    )
    scores = jnp.where(valid, scores, -jnp.inf)
    own = (
        jnp.einsum("rgd,rd->rg", queries, new_keys[:, 0], preferred_element_type=jnp.float32)
        * scale
    )
    peak = jnp.maximum(jnp.max(scores, axis=-1), own)
    weights = jnp.exp(scores - peak[..., None])
    own_weight = jnp.exp(own - peak)
    total = jnp.sum(weights, axis=-1) + own_weight
    probs = (weights / total[..., None]).astype(jnp.bfloat16)
    own_prob = (own_weight / total).astype(jnp.bfloat16)
    result = jnp.einsum("rgl,rld->rgd", probs, cached_values, preferred_element_type=jnp.float32)
    result = (
        result
        + own_prob.astype(jnp.float32)[..., None] * new_values[:, 0].astype(jnp.float32)[:, None, :]
    )
    attended = result.reshape(result.shape[0], -1).astype(jnp.bfloat16)
    mine = lax.all_to_all(attended, "role", split_axis=0, concat_axis=1, tiled=True)
    tokens, width = mine.shape
    wide = mine.astype(jnp.float32)
    normed = (
        wide * lax.rsqrt(jnp.mean(wide * wide, axis=-1, keepdims=True) + 1e-06) * norm_gain
    ).astype(jnp.bfloat16)
    first = lax.axis_index("role") * tokens
    ids = lax.dynamic_slice_in_dim(expert_ids, first, tokens, 0)
    scores_kept = lax.dynamic_slice_in_dim(route_weights, first, tokens, 0)
    share = (scores_kept / jnp.sum(scores_kept, axis=-1, keepdims=True)).reshape(-1)
    top = ids.shape[1]
    ids = ids.reshape(-1)
    n_role = lax.axis_size("role")
    n_dev = lax.axis_size("dev")
    experts = n_role * n_dev
    capacity = max(2, 3 * tokens * top // (2 * experts))
    position = jnp.arange(ids.shape[0], dtype=jnp.int32)
    earlier = jnp.sum(
        ((ids[None, :] == ids[:, None]) & (position[None, :] < position[:, None])).astype(
            jnp.int32
        ),
        axis=1,
    )
    target = ids * capacity + earlier
    hits = jnp.arange(experts * capacity, dtype=jnp.int32)[:, None] == target[None, :]
    by_token = jnp.any(hits.reshape(experts * capacity, tokens, top), axis=2).astype(jnp.bfloat16)
    outgoing = (
        jnp.dot(by_token, normed, preferred_element_type=jnp.float32)
        .astype(jnp.bfloat16)
        .reshape(experts, capacity, width)
    )
    produced = run_expert(
        lax.all_to_all(outgoing, ("role", "dev"), split_axis=0, concat_axis=0, tiled=True),
        gate_weight,
        up_weight,
        down_weight,
    )
    back = lax.all_to_all(produced, ("role", "dev"), split_axis=0, concat_axis=0, tiled=True)
    per_route = jnp.dot(
        hits.T.astype(jnp.bfloat16),
        back.reshape(experts * capacity, width),
        preferred_element_type=jnp.float32,
    )
    moe = jnp.sum((per_route * share[:, None]).reshape(tokens, top, width), axis=1)
    mixed = (wide + moe).astype(jnp.bfloat16)
    return mixed.reshape(1, 1, tokens, width)


def solution(mesh):
    return jax.shard_map(
        per_device,
        mesh=mesh,
        in_specs=(
            P("dev", "role", None),
            P("dev", "role", None, None),
            P("dev", "role", None, None),
            P("dev", "role", None),
            P("dev", "role", None),
            P("dev"),
            P(),
            P("dev", None),
            P("dev", None),
            P(("role", "dev"), None, None),
            P(("role", "dev"), None, None),
            P(("role", "dev"), None, None),
        ),
        out_specs=P("dev", "role", None, None),
        check_vma=False,
    )
```

profile of v0, /device:TPU:1, one launch (start us, length us, event | category | flops | bytes accessed | tf_op | source)
XLA Modules:
  0.0 125.6 jit_solution(3175292428846809118)
XLA Ops:
  0.0 0.9 iota_compare_fusion.4
  0.9 0.8 bitcast_convert_fusion
  1.7 1.1 fusion.46
  2.7 1.9 %fusion.51 = (f32[32,16]{1,0:T(8,128)S(1)}, f32[32,16,192]{2,1,0:T(8,128)S(1)}) fusion(bf16[32,16,128]{2,1,0:T(8,128)(2,1)} %param.12, bf16[32,1,192,128]{3,2,1,0:T(8,128)(2,1)S(1)} %copy-done, pred[32,192]{1,0:T(8,128)(4,1)S(1)} %iota_compare_fusion.4), kind=kOutput, calls=%fused_computation.59 | convolution fusion | flops 25460224 | bytes 2105344 | tf_op jit(solution)/shard_map/rgd,rld->rgl/dot_general | solution.py:37
  4.7 0.3 fusion.35
  5.0 0.6 fusion.30
  5.6 0.7 convert_element_type.75
  6.3 4.8 %all-to-all-start = ((bf16[2,16,2048]{2,1,0:T(8,128)(2,1)}), bf16[2,16,2048]{2,1,0:T(8,128)(2,1)S(1)}, u32[]{:S(2)}, u32[]{:S(2)}) async-start(bf16[2,16,2048]{2,1,0:T(8,128)(2,1)} %convert_element_type.75), calls=%async_computation | async-start | bytes 262144 | tf_op jit(solution)/shard_map/all_to_all | solution.py:59
  11.2 0.1 copy.32
  11.3 0.1 reshape.104
  11.3 0.2 convert_reduce_fusion
  11.5 0.1 reduce_sum.51
  11.6 0.1 fusion.43
  11.8 0.5 all-to-all-done
  12.2 0.1 fusion.37
  12.5 2.0 %convolution_convert_fusion = bf16[256,4096]{1,0:T(8,128)(2,1)} fusion(pred[256,16]{0,1:T(8,128)(4,1)S(1)} %fusion.43, f32[16,4096]{1,0:T(8,128)S(1)} %bitcast.59, f32[4096]{0:T(1024)S(1)} %copy-done.1, f32[16]{0:T(128)S(1)} %add_rsqrt_fusion), kind=kOutput, calls=%fused_computation.6 | convolution fusion | flops 34799616 | bytes 2379840 | tf_op jit(solution)/shard_map/dot_general | solution.py:86
  14.5 4.4 %reshape.105 = bf16[128,2,4096]{2,1,0:T(2,128)(2,1)} reshape(bf16[256,4096]{1,0:T(8,128)(2,1)} %convolution_convert_fusion) | data formatting | bytes 4194304 | tf_op jit(solution)/shard_map/reshape | solution.py:88
  18.9 39.3 %all_to_all.20 = bf16[128,2,4096]{2,1,0:T(2,128)(2,1)} all-to-all(bf16[128,2,4096]{2,1,0:T(2,128)(2,1)} %reshape.105), channel_id=1, replica_groups=mesh['role'=2,'dev'=64] {'role','dev'}, dimensions={0} | all-to-all | bytes 4194304 | tf_op jit(solution)/shard_map/all_to_all | solution.py:91
  58.2 4.1 %reshape.106 = bf16[256,4096]{1,0:T(8,128)(2,1)} reshape(bf16[128,2,4096]{2,1,0:T(2,128)(2,1)} %all_to_all.20) | data formatting | bytes 4194304 | tf_op jit(solution)/shard_map/reshape | solution.py:11
  62.3 5.2 %fusion.4 = f32[256,768]{1,0:T(8,128)S(1)} fusion(bf16[256,4096]{1,0:T(8,128)(2,1)} %reshape.106, bf16[1,4096,768]{2,1,0:T(8,128)(2,1)} %param.21), kind=kOutput, calls=%fused_computation.4 | convolution fusion | flops 1610612736 | bytes 9175040 | tf_op jit(solution)/shard_map/dot_general | solution.py:12
  67.5 11.1 %fusion.6 = bf16[256,4096]{1,0:T(8,128)(2,1)} fusion(bf16[1,768,4096]{2,1,0:T(8,128)(2,1)} %param.23, bf16[256,4096]{1,0:T(8,128)(2,1)} %reshape.106, bf16[1,4096,768]{2,1,0:T(8,128)(2,1)} %param.22, f32[256,768]{1,0:T(8,128)S(1)} %fusion.4), kind=kOutput, calls=%fused_computation.7 | convolution fusion | flops 3223453696 | bytes 17563648 | tf_op jit(solution)/shard_map/dot_general | solution.py:15
  78.6 4.4 %reshape.107 = bf16[128,2,4096]{2,1,0:T(2,128)(2,1)} reshape(bf16[256,4096]{1,0:T(8,128)(2,1)} %fusion.6) | data formatting | bytes 4194304 | tf_op jit(solution)/shard_map/reshape | solution.py:16
  83.0 6.8 %all-to-all-start.2 = ((bf16[128,2,4096]{2,1,0:T(2,128)(2,1)}), bf16[128,2,4096]{2,1,0:T(2,128)(2,1)}, u32[]{:S(2)}, u32[]{:S(2)}) async-start(bf16[128,2,4096]{2,1,0:T(2,128)(2,1)} %reshape.107), calls=%async_computation.2 | async-start | bytes 4194304 | tf_op jit(solution)/shard_map/all_to_all | solution.py:96
  89.9 0.1 dynamic-slice_reduce_fusion
  90.0 0.1 copy.29
  90.1 0.1 mul.107
  90.2 0.2 copy.26
  90.4 0.2 reshape.111
  90.7 27.6 %all-to-all-done.2 = bf16[128,2,4096]{2,1,0:T(2,128)(2,1)} async-done(((bf16[128,2,4096]{2,1,0:T(2,128)(2,1)}), bf16[128,2,4096]{2,1,0:T(2,128)(2,1)}, u32[]{:S(2)}, u32[]{:S(2)}) %all-to-all-start.2) | async-done | bytes 2097184 | tf_op jit(solution)/shard_map/all_to_all | solution.py:96
  118.2 4.1 %reshape.108 = bf16[256,4096]{1,0:T(8,128)(2,1)} reshape(bf16[128,2,4096]{2,1,0:T(2,128)(2,1)} %all-to-all-done.2) | data formatting | bytes 4194304 | tf_op jit(solution)/shard_map/reshape | solution.py:99
  122.4 2.5 %fusion.14 = f32[16,4096]{1,0:T(8,128)S(1)} fusion(bf16[256,4096]{1,0:T(8,128)(2,1)} %reshape.108, f32[128]{0:T(128)S(1)} %mul.107, s32[128]{0:T(128)S(1)} %multiply_add_fusion.1), kind=kOutput, calls=%fused_computation.14 | convolution fusion | flops 269451264 | bytes 2360320 | tf_op jit(solution)/shard_map/dot_general | solution.py:97
  124.9 0.7 fusion.38
  (19 shorter events, 0.3 us)
Async XLA Ops:
  0.0 2.7 %copy-start = (bf16[32,1,192,128]{3,2,1,0:T(8,128)(2,1)S(1)}, bf16[32,1,192,128]{3,2,1,0:T(8,128)(2,1)}, u32[]{:S(2)}) copy-start(bf16[32,1,192,128]{3,2,1,0:T(8,128)(2,1)} %param.13) | copy-start | bytes 4718596
  0.0 5.0 %copy-start.4 = (bf16[32,1,192,128]{3,2,1,0:T(8,128)(2,1)S(1)}, bf16[32,1,192,128]{3,2,1,0:T(8,128)(2,1)}, u32[]{:S(2)}) copy-start(bf16[32,1,192,128]{3,2,1,0:T(8,128)(2,1)} %param.14) | copy-start | bytes 4718596
  4.9 6.2 %copy-start.3 = (s32[32,8]{0,1:T(8,128)S(1)}, s32[32,8]{0,1:T(8,128)}, u32[]{:S(2)}) copy-start(s32[32,8]{0,1:T(8,128)} %param.19) | copy-start | bytes 3076
  5.0 7.5 %copy-start.1 = (f32[4096]{0:T(1024)S(1)}, f32[4096]{0:T(1024)}, u32[]{:S(2)}) copy-start(f32[4096]{0:T(1024)} %param.18) | copy-start | bytes 49156
  6.3 5.9 %all-to-all-start = ((bf16[2,16,2048]{2,1,0:T(8,128)(2,1)}), bf16[2,16,2048]{2,1,0:T(8,128)(2,1)S(1)}, u32[]{:S(2)}, u32[]{:S(2)}) async-start(bf16[2,16,2048]{2,1,0:T(8,128)(2,1)} %convert_element_type.75), calls=%async_computation | async-start | bytes 262144 | tf_op jit(solution)/shard_map/all_to_all | solution.py:59
  83.0 6.9 %copy-start.2 = (f32[32,8]{0,1:T(8,128)S(1)}, f32[32,8]{0,1:T(8,128)}, u32[]{:S(2)}) copy-start(f32[32,8]{0,1:T(8,128)} %param.20) | copy-start | bytes 3076
  83.0 35.3 %all-to-all-start.2 = ((bf16[128,2,4096]{2,1,0:T(2,128)(2,1)}), bf16[128,2,4096]{2,1,0:T(2,128)(2,1)}, u32[]{:S(2)}, u32[]{:S(2)}) async-start(bf16[128,2,4096]{2,1,0:T(2,128)(2,1)} %reshape.107), calls=%async_computation.2 | async-start | bytes 4194304 | tf_op jit(solution)/shard_map/all_to_all | solution.py:96
where the time goes:
time: 126 us
  blocking collectives  39.3 us (31%)
  waiting for transfers between devices  28.1 us (22%)
  matrix products  24.4 us (19%)
  local copies, waits for them, and re-layouts  18.7 us (15%)
  starting transfers between devices  11.6 us (9%)
  other arithmetic  3.32 us (3%)
    all_to_all x1, blocking collectives, per_device(): lax.all_to_all(outgoing, ('role', 'dev'), split_axis=0, concat_axis=0, ti...  39.3 us
    all_to_all x1, waiting for transfers between devices, per_device(): lax.all_to_all(produced, ('role', 'dev'), split_axis=0, concat_axis=0, ti...  27.6 us
    dot_general x1, matrix products, run_expert(): out = jnp.dot(hidden, down_weight[0], preferred_element_type=jnp.float32)  11.1 us
    all_to_all x1, starting transfers between devices, per_device(): lax.all_to_all(produced, ('role', 'dev'), split_axis=0, concat_axis=0, ti...  6.85 us
    dot_general x1, matrix products, run_expert(): gate = jnp.dot(flat, gate_weight[0], preferred_element_type=jnp.float32)  5.2 us
    all_to_all x1, starting transfers between devices, per_device(): lax.all_to_all(attended, 'role', split_axis=0, concat_axis=1, tiled=True)  4.79 us
    reshape x1, local copies, waits for them, and re-layouts, run_expert(): return out.astype(jnp.bfloat16).reshape(sources, slots, width)  4.4 us
    reshape x1, local copies, waits for them, and re-layouts, per_device(): outgoing = jnp.dot(by_token, normed, preferred_element_type=jnp.float32)....  4.39 us
  transfers between devices with their start and end apart: 2, of which 2 were waited for; matrix products, arithmetic and copies ran while one was open for 1% of the time, Pallas kernels for 0%

commit v1 on v0

v1 whole, which is shorter than its diff:
```python
import jax
import jax.numpy as jnp
from jax import lax
from jax.experimental import pallas as pl
from jax.experimental.pallas import tpu as pltpu
from jax.sharding import PartitionSpec as P

HEAD = 128
HEADS = 16
TOK = 32
LEN = 192
LEN_PAD = 208
HALF = 2048
WIDTH = 4096
FF = 768
EXPERTS = 128
STRIDES = (16, 4, 1)
ORDERS = ((1, 0, 2), (0, 2, 1), (2, 1, 0))
CHUNKS = ((384, 384, 256), (384, 256, 384))
PIECES = []
for _j, _sizes in enumerate(CHUNKS):
    _at = _j * 1024
    for _k, _size in enumerate(_sizes):
        PIECES.append((_j, _k, _at, _size))
        _at += _size
N = len(PIECES)
MESH = pl.DeviceIdType.MESH
BF = jnp.bfloat16
F32 = jnp.float32


def rows_dot(a, b):
    return lax.dot_general(a, b, (((1,), (1,)), ((), ())), preferred_element_type=F32)


def dot(a, b):
    return jnp.dot(a, b, preferred_element_type=F32)


def kernel(
    lengths,
    ids,
    route,
    gain,
    queries,
    new_keys,
    new_values,
    keys_hbm,
    values_hbm,
    gate_hbm,
    up_hbm,
    down_hbm,
    out,
    *scratch,
):
    refs = list(scratch)

    def take(count):
        taken = refs[:count]
        del refs[:count]
        return taken

    gathered, picked, arrived, produced, returned, partial, parts, summed, pieces = (
        take(N) for _ in range(9)
    )
    meta = take(3)
    (keys, values, heads, gate_w, up_w, down_w, normed, gate, up, hidden, squares) = take(11)
    select, combine, other, mixed = take(4)
    (load_sem, weight_sem, meta_sem, g1_sem, g2_sem, ex_sem, back_sem, r1_sem, r2_sem, swap_sem) = (
        take(10)
    )

    role = lax.axis_index("role")
    dev = lax.axis_index("dev")
    here = (dev // 16, (dev // 4) % 4, dev % 4)

    def at(axis, value):
        return dev + (value - here[axis]) * STRIDES[axis]

    def along(axis, step):
        return lax.rem(here[axis] + step, 4)

    def send(src, dst, sems, index, target):
        pltpu.make_async_remote_copy(
            src_ref=src,
            dst_ref=dst,
            send_sem=sems.at[0, index],
            recv_sem=sems.at[1, index],
            device_id=target,
            device_id_type=MESH,
        ).start()

    def settle(ref, sem):
        pltpu.make_async_copy(ref, ref, sem).wait()

    loads = []
    for part in range(2):
        span = pl.ds(part * 16, 16)
        for n, (src, dst) in enumerate(((keys_hbm, keys), (values_hbm, values))):
            copy = pltpu.make_async_copy(
                src.at[span, 0], dst.at[span, pl.ds(0, LEN)], load_sem.at[part, n]
            )
            copy.start()
            loads.append(copy)
    weights = []
    for n, (src, dst) in enumerate(((gate_hbm, gate_w), (up_hbm, up_w), (down_hbm, down_w))):
        copy = pltpu.make_async_copy(src.at[0], dst, weight_sem.at[n])
        copy.start()
        weights.append(copy)

    barrier = pltpu.get_barrier_semaphore()
    for axis in range(3):
        for step in (1, 2, 3):
            for who in range(2):
                pl.semaphore_signal(
                    barrier, inc=1, device_id=(who, at(axis, along(axis, step))), device_id_type=MESH
                )
    pl.semaphore_signal(barrier, inc=1, device_id=(1 - role, dev), device_id_type=MESH)

    lane = lax.broadcasted_iota(jnp.int32, (TOK, EXPERTS), 1)
    share = route[...] / jnp.sum(route[...], axis=1, keepdims=True)
    named = ids[...]
    hit = jnp.zeros((TOK, EXPERTS), F32)
    shares = jnp.zeros((TOK, EXPERTS), F32)
    for k in range(named.shape[1]):
        same = named[:, k : k + 1] == lane
        hit = jnp.where(same, 1.0, hit)
        shares = jnp.where(same, share[:, k : k + 1], shares)
    row = lax.broadcasted_iota(jnp.int32, (TOK, TOK), 0)
    col = lax.broadcasted_iota(jnp.int32, (TOK, TOK), 1)
    before = jnp.where((row // 16 == col // 16) & (col < row), 1.0, 0.0).astype(BF)
    second = dot(before, hit.astype(BF))
    signed = jnp.where(second > 0.5, -shares, shares).astype(BF)
    for k, (a1, a2, _) in enumerate(ORDERS):
        meta[k][here[a2], here[a1]] = signed

    scale = HEAD ** (-0.5)
    first_row = lax.broadcasted_iota(jnp.int32, (16, HEAD), 0) == 0
    place = lax.broadcasted_iota(jnp.int32, (HEADS, LEN_PAD), 1)

    def attend(first):
        probs = []
        for n in range(8):
            r = first + n
            own_key = jnp.broadcast_to(new_keys[r], (16, HEAD)).astype(F32)
            own_value = jnp.broadcast_to(new_values[r], (16, HEAD)).astype(F32)
            keys[r, LEN:LEN_PAD, :] = jnp.where(first_row, own_key, 0.0).astype(BF)
            values[r, LEN:LEN_PAD, :] = jnp.where(first_row, own_value, 0.0).astype(BF)
            scores = rows_dot(queries[r], keys[r]) * scale
            live = (place < lengths[r]) | (place == LEN)
            probs.append(jnp.where(live, scores, -jnp.inf))
        scores = jnp.concatenate(probs, axis=0)
        spread = jnp.exp(scores - jnp.max(scores, axis=1, keepdims=True))
        spread = (spread / jnp.sum(spread, axis=1, keepdims=True)).astype(BF)
        for n in range(8):
            r = first + n
            start = pl.multiple_of(r * HEADS, HEADS)
            heads[pl.ds(start, HEADS), :] = dot(spread[n * HEADS : (n + 1) * HEADS], values[r])

    def attend_half(part):
        def step(n, carry):
            attend(part * 16 + n * 8)
            return carry

        loads[2 * part].wait()
        loads[2 * part + 1].wait()
        lax.fori_loop(0, 2, step, 0)

    attend_half(0)
    pl.semaphore_wait(barrier, 19)
    for k, (a1, a2, _) in enumerate(ORDERS):
        for step in (2, 1, 3):
            block = meta[k].at[here[a2], here[a1]]
            send(block, block, meta_sem, k, (role, at(a1, along(a1, step))))
    attend_half(1)

    for i, (_, k, first, size) in enumerate(PIECES):
        a1, a2, _ = ORDERS[k]
        for h in range(size // HEAD):
            head = first // HEAD + h
            gathered[i][here[a2], here[a1], :, h * HEAD : (h + 1) * HEAD] = heads[
                pl.ds(head, TOK, stride=HEADS), :
            ].astype(BF)
        for step in (2, 1, 3):
            block = gathered[i].at[here[a2], here[a1]]
            send(block, block, g1_sem, i, (role, at(a1, along(a1, step))))

    for k, (a1, a2, _) in enumerate(ORDERS):
        settle(meta[k].at[0, pl.ds(0, 3)], meta_sem.at[1, k])
        for step in (2, 1, 3):
            block = meta[k].at[here[a2]]
            send(block, block, meta_sem, 3 + k, (role, at(a2, along(a2, step))))

    for i, (_, k, _, _) in enumerate(PIECES):
        a1, a2, _ = ORDERS[k]
        settle(gathered[i].at[0, pl.ds(0, 3)], g1_sem.at[1, i])
        for step in (2, 1, 3):
            block = gathered[i].at[here[a2]]
            send(block, block, g2_sem, i, (role, at(a2, along(a2, step))))

    row = lax.broadcasted_iota(jnp.int32, (128, 128), 0)
    col = lax.broadcasted_iota(jnp.int32, (128, 128), 1)
    for k, (_, _, a3) in enumerate(ORDERS):
        settle(meta[k].at[pl.ds(0, 3)], meta_sem.at[1, 3 + k])
        expert = ((row // 16) % 2) * 64 + at(a3, row // 32)
        chosen = jnp.where(expert == col, 1.0, 0.0).astype(BF)
        for b in range(4):
            marks = meta[k][b].reshape(128, EXPERTS)
            wide = rows_dot(chosen, marks)
            wide = jnp.where(row % 2 == 0, wide, -wide)
            mask = ((row % 16) // 2 == col // 16) & (wide > 0.0)
            select[k, b] = jnp.where(mask, 1.0, 0.0).astype(BF)
            tall = rows_dot(marks, chosen)
            tall = jnp.where(col % 2 == 0, tall, -tall)
            mask = ((col % 16) // 2 == row // 16) & (tall > 0.0)
            combine[k, b] = jnp.where(mask, tall, 0.0).astype(BF)

    for i, (_, k, _, size) in enumerate(PIECES):
        a3 = ORDERS[k][2]
        settle(gathered[i].at[pl.ds(0, 3)], g2_sem.at[1, i])
        for b in range(4):
            rows = dot(select[k, b], gathered[i][b].reshape(128, size)).astype(BF)
            picked[i][:, b * 16 : (b + 1) * 16, :] = rows.reshape(8, 16, size)
        for step in (2, 1, 3):
            there = along(a3, step)
            for who in range(2):
                send(
                    picked[i].at[there * 2 + who],
                    arrived[i].at[role, here[a3]],
                    ex_sem,
                    i,
                    (who, at(a3, there)),
                )
        send(
            picked[i].at[here[a3] * 2 + 1 - role],
            arrived[i].at[role, here[a3]],
            ex_sem,
            i,
            (1 - role, dev),
        )
        pltpu.make_async_copy(
            picked[i].at[here[a3] * 2 + role], arrived[i].at[role, here[a3]], ex_sem.at[1, i]
        ).start()

    row = lax.broadcasted_iota(jnp.int32, (256, 256), 0)
    col = lax.broadcasted_iota(jnp.int32, (256, 256), 1)

    def common(index):
        a1, a2, a3 = ORDERS[0]
        place = {a3: index // 64, a2: (index // 16) % 4, a1: (index // 4) % 4}
        return place

    def turned(index, k):
        place = common(index)
        a1, a2, a3 = ORDERS[k]
        return place[a3] * 64 + place[a2] * 16 + place[a1] * 4 + index % 4

    squares[...] = jnp.zeros_like(squares)
    gate[...] = jnp.zeros_like(gate)
    up[...] = jnp.zeros_like(up)
    weights[0].wait()
    weights[1].wait()
    for j in range(len(CHUNKS)):
        for i, (chunk, k, first, size) in enumerate(PIECES):
            if chunk != j:
                continue
            settle(arrived[i], ex_sem.at[1, i])
            for c in range(2):
                rows = arrived[i][c].reshape(256, size)
                if k == 0:
                    rows = rows.astype(F32)
                else:
                    rows = dot(jnp.where(turned(row, k) == col, 1.0, 0.0).astype(BF), rows)
                begin = c * HALF + first
                total = squares[...]
                for t in range(size // HEAD):
                    tile = rows[:, t * HEAD : (t + 1) * HEAD]
                    total = total + tile * tile
                squares[...] = total
                normed[:, begin : begin + size] = (rows * gain[:, begin : begin + size]).astype(BF)
        for c in range(2):
            begin = c * HALF + j * 1024

            def tile(n, carry, begin=begin):
                cols = pl.ds(pl.multiple_of(n * 256, 256), 256)
                left = normed[:, begin : begin + 1024]
                gate[:, cols] += dot(left, gate_w[begin : begin + 1024, cols])
                up[:, cols] += dot(left, up_w[begin : begin + 1024, cols])
                return carry

            lax.fori_loop(0, FF // 256, tile, 0)

    factor = lax.rsqrt(jnp.sum(squares[...], axis=1, keepdims=True) * (1.0 / WIDTH) + 1e-06)
    gated = gate[...] * factor
    hidden[0] = (gated / (1.0 + jnp.exp(-gated)) * (up[...] * factor)).astype(BF)
    for k in (1, 2):
        turn = jnp.where(turned(col, k) == row, 1.0, 0.0).astype(BF)
        hidden[k] = dot(turn, hidden[0]).astype(BF)

    weights[2].wait()
    for i, (_, k, first, size) in enumerate(PIECES):
        a3 = ORDERS[k][2]
        for c in range(2):
            begin = c * HALF + first
            rows = dot(hidden[k], down_w[:, begin : begin + size]).astype(BF)
            produced[i][c] = rows.reshape(4, 64, size)
        for step in (2, 1, 3):
            there = along(a3, step)
            for who in range(2):
                send(
                    produced[i].at[who, there],
                    returned[i].at[here[a3] * 2 + role],
                    back_sem,
                    i,
                    (who, at(a3, there)),
                )
        send(
            produced[i].at[1 - role, here[a3]],
            returned[i].at[here[a3] * 2 + role],
            back_sem,
            i,
            (1 - role, dev),
        )
        pltpu.make_async_copy(
            produced[i].at[role, here[a3]],
            returned[i].at[here[a3] * 2 + role],
            back_sem.at[1, i],
        ).start()

    for i, (_, k, _, size) in enumerate(PIECES):
        a2 = ORDERS[k][1]
        settle(returned[i], back_sem.at[1, i])
        for b in range(4):
            rows = returned[i][:, b * 16 : (b + 1) * 16, :].reshape(128, size)
            partial[i][b] = dot(combine[k, b], rows).astype(BF)
        for step in (2, 1, 3):
            there = along(a2, step)
            send(
                partial[i].at[there], parts[i].at[here[a2]], r1_sem, i, (role, at(a2, there))
            )
        pltpu.make_async_copy(
            partial[i].at[here[a2]], parts[i].at[here[a2]], r1_sem.at[1, i]
        ).start()

    for i, (_, k, _, size) in enumerate(PIECES):
        a1 = ORDERS[k][0]
        settle(parts[i], r1_sem.at[1, i])
        total = parts[i][0].astype(F32)
        for b in range(1, 4):
            total = total + parts[i][b].astype(F32)
        summed[i][...] = total.astype(BF).reshape(4, TOK, size)
        for step in (2, 1, 3):
            there = along(a1, step)
            send(
                summed[i].at[there], pieces[i].at[here[a1]], r2_sem, i, (role, at(a1, there))
            )
        pltpu.make_async_copy(
            summed[i].at[here[a1]], pieces[i].at[here[a1]], r2_sem.at[1, i]
        ).start()

    for i, (_, k, first, size) in enumerate(PIECES):
        a1, a2, _ = ORDERS[k]
        settle(pieces[i], r2_sem.at[1, i])
        total = pieces[i][0].astype(F32)
        for b in range(1, 4):
            total = total + pieces[i][b].astype(F32)
        total = total + gathered[i][here[a2], here[a1]].astype(F32)
        mixed[:, :, first : first + size] = total.astype(BF).reshape(2, 16, size)
    swap = pltpu.make_async_remote_copy(
        src_ref=mixed.at[1 - role],
        dst_ref=other,
        send_sem=swap_sem.at[0],
        recv_sem=swap_sem.at[1],
        device_id=(1 - role, dev),
        device_id_type=MESH,
    )
    swap.start()
    out[:, pl.ds(pl.multiple_of(role * HALF, HALF), HALF)] = mixed[role]
    swap.wait()
    out[:, pl.ds(pl.multiple_of((1 - role) * HALF, HALF), HALF)] = other[...]

    for k in range(3):
        settle(meta[k].at[0, pl.ds(0, 3)], meta_sem.at[0, k])
        settle(meta[k].at[pl.ds(0, 3)], meta_sem.at[0, 3 + k])
    for i in range(N):
        settle(gathered[i].at[0, pl.ds(0, 3)], g1_sem.at[0, i])
        settle(gathered[i].at[pl.ds(0, 3)], g2_sem.at[0, i])
        settle(picked[i].at[pl.ds(0, 7)], ex_sem.at[0, i])
        settle(picked[i].at[pl.ds(0, 7)], back_sem.at[0, i])
        settle(partial[i].at[pl.ds(0, 3)], r1_sem.at[0, i])
        settle(summed[i].at[pl.ds(0, 3)], r2_sem.at[0, i])


def per_device(
    queries,
    keys_cache,
    values_cache,
    new_keys,
    new_values,
    lengths,
    norm_gain,
    expert_ids,
    route_weights,
    gate_weight,
    up_weight,
    down_weight,
):
    sizes = [size for _, _, _, size in PIECES]

    def buffers(*lead):
        return [pltpu.VMEM((*lead, size), BF) for size in sizes]

    vmem = pl.BlockSpec(memory_space=pltpu.VMEM)
    hbm = pl.BlockSpec(memory_space=pl.ANY)
    mixed = pl.pallas_call(
        kernel,
        name="layer",
        out_shape=jax.ShapeDtypeStruct((16, WIDTH), BF),
        in_specs=[pl.BlockSpec(memory_space=pltpu.SMEM)] + [vmem] * 6 + [hbm] * 5,
        out_specs=vmem,
        scratch_shapes=[
            *buffers(4, 4, TOK),
            *buffers(8, 64),
            *buffers(2, 4, 64),
            *buffers(2, 4, 64),
            *buffers(8, 64),
            *buffers(4, 128),
            *buffers(4, 128),
            *buffers(4, TOK),
            *buffers(4, TOK),
            *[pltpu.VMEM((4, 4, TOK, EXPERTS), BF)] * 3,
            pltpu.VMEM((TOK, LEN_PAD, HEAD), BF),
            pltpu.VMEM((TOK, LEN_PAD, HEAD), BF),
            pltpu.VMEM((TOK * HEADS, HEAD), F32),
            pltpu.VMEM((WIDTH, FF), BF),
            pltpu.VMEM((WIDTH, FF), BF),
            pltpu.VMEM((FF, WIDTH), BF),
            pltpu.VMEM((256, WIDTH), BF),
            pltpu.VMEM((256, FF), F32),
            pltpu.VMEM((256, FF), F32),
            pltpu.VMEM((3, 256, FF), BF),
            pltpu.VMEM((256, HEAD), F32),
            pltpu.VMEM((3, 4, 128, 128), BF),
            pltpu.VMEM((3, 4, 128, 128), BF),
            pltpu.VMEM((16, HALF), BF),
            pltpu.VMEM((2, 16, HALF), BF),
            pltpu.SemaphoreType.DMA((2, 2)),
            pltpu.SemaphoreType.DMA((3,)),
            pltpu.SemaphoreType.DMA((2, 6)),
            *[pltpu.SemaphoreType.DMA((2, N))] * 6,
            pltpu.SemaphoreType.DMA((2,)),
        ],
        compiler_params=pltpu.CompilerParams(
            collective_id=0, has_side_effects=True, vmem_limit_bytes=60 * 2**20
        ),
        cost_estimate=pl.CostEstimate(
            flops=6 * 256 * WIDTH * FF, bytes_accessed=22 * 2**20, transcendentals=0
        ),
    )(
        lengths,
        expert_ids,
        route_weights,
        norm_gain.reshape(1, WIDTH),
        queries,
        new_keys,
        new_values,
        keys_cache,
        values_cache,
        gate_weight,
        up_weight,
        down_weight,
    )
    return mixed.reshape(1, 1, 16, WIDTH)


def solution(mesh):
    return jax.shard_map(
        per_device,
        mesh=mesh,
        in_specs=(
            P("dev", "role", None),
            P("dev", "role", None, None),
            P("dev", "role", None, None),
            P("dev", "role", None),
            P("dev", "role", None),
            P("dev"),
            P(),
            P("dev", None),
            P("dev", None),
            P(("role", "dev"), None, None),
            P(("role", "dev"), None, None),
            P(("role", "dev"), None, None),
        ),
        out_specs=P("dev", "role", None, None),
        check_vma=False,
    )
```

time: 126 us -> 72.7 us (0.58)
  Pallas kernels: 0 us -> 65.5 us
  blocking collectives: 39.3 us -> 0 us
  waiting for transfers between devices: 28.1 us -> 0 us
  matrix products: 24.4 us -> 0 us
  local copies, waits for them, and re-layouts: 18.7 us -> 6.9 us
  starting transfers between devices: 11.6 us -> 0 us
  other arithmetic: 3.32 us -> 0 us
    pallas_call x0 -> x1, Pallas kernels: none -> 65.5 us  [per_device(): pl.pallas_call(kernel, name='layer', out_shape=jax.ShapeDtypeStruct((16,...]
    all_to_all x1 -> x0, blocking collectives: 39.3 us -> none  [per_device(): lax.all_to_all(outgoing, ('role', 'dev'), split_axis=0, concat_axis=0, ti...]
    all_to_all x2 -> x0, waiting for transfers between devices: 28.1 us -> none  [the longest x1 27.6 us: per_device(): lax.all_to_all(produced, ('role', 'dev'), split_axis=0, concat_axis=0, ti...]
    dot_general x7 -> x0, matrix products: 24.4 us -> none  [the longest x1 11.1 us: run_expert(): out = jnp.dot(hidden, down_weight[0], preferred_element_type=jnp.float32)]
    reshape x5 -> x0, local copies, waits for them, and re-layouts: 17.1 us -> none  [the longest x1 4.4 us: run_expert(): return out.astype(jnp.bfloat16).reshape(sources, slots, width)]
    all_to_all x2 -> x0, starting transfers between devices: 11.6 us -> none  [the longest x1 6.85 us: per_device(): lax.all_to_all(produced, ('role', 'dev'), split_axis=0, concat_axis=0, ti...]
    unnamed x11 -> x5, local copies, waits for them, and re-layouts: 0.1 us -> 6.9 us
  transfers between devices with their start and end apart: 2 -> 0, of which waited for: 2 -> 0; matrix products, arithmetic and copies ran while one was open for 1% -> 0% of each run, Pallas kernels for 0% -> 0%
where the time goes in v1:
time: 72.7 us; the launch traced here: 72.4 us
  Pallas kernels  65.5 us (90%)
  local copies, waits for them, and re-layouts  6.9 us (9%)
    pallas_call x1, Pallas kernels, per_device(): pl.pallas_call(kernel, name='layer', out_shape=jax.ShapeDtypeStruct((16,...  65.5 us
    unnamed x5, local copies, waits for them, and re-layouts  6.9 us

profile of v1, /device:TPU:1, one launch (start us, length us, event | category | flops | bytes accessed | tf_op | source)
XLA Modules:
  0.0 72.4 jit_solution(3764490282556388667)
XLA Ops:
  0.0 1.3 %copy.15.new_keys = bf16[32,1,128]{2,1,0:T(2,128)(2,1)} copy(bf16[32,1,128]{2,0,1:T(8,128)(2,1)} %param.15) | data formatting | bytes 16384 | tf_op args[3]
  1.3 1.3 %copy.16.new_values = bf16[32,1,128]{2,1,0:T(2,128)(2,1)} copy(bf16[32,1,128]{2,0,1:T(8,128)(2,1)} %param.16) | data formatting | bytes 16384 | tf_op args[4]
  2.6 1.4 %copy.13.ids = s32[32,8]{1,0:T(8,128)} copy(s32[32,8]{0,1:T(8,128)} %param.19) | data formatting | bytes 2048 | tf_op args[7]
  4.0 1.4 %copy.14.route = f32[32,8]{1,0:T(8,128)} copy(f32[32,8]{0,1:T(8,128)} %param.20) | data formatting | bytes 2048 | tf_op args[8]
  5.3 65.5 %layer.1 = bf16[16,4096]{1,0:T(8,128)(2,1)} custom-call(s32[32]{0:T(128)} %lengths.1, s32[32,8]{1,0:T(8,128)} %copy.13.ids, f32[32,8]{1,0:T(8,128)} %copy.14.route, f32[1,4096]{1,0:T(1,128)} %bitcast.3, bf16[32,16,128]{2,1,0:T(8,128)(2,1)} %queries.1, bf16[32,1,128]{2,1,0:T(2,128)(2,1)} %copy.15.new_keys, bf16[32,1,128]{2,1,0:T(2,128)(2,1)} %copy.16.new_values, ...), custom_call_target="tpu_custom_call" | custom-call | flops 4831838208 | bytes 23068672 | tf_op jit(solution)/shard_map/layer/pallas_call | solution.py:415
  70.8 1.6 %copy.18 = bf16[1,1,16,4096]{3,2,1,0:T(8,128)(2,1)} copy(bf16[1,1,16,4096]{3,2,1,0:T(8,128)(2,1)} %bitcast.2) | data formatting | bytes 262144

commit v2 on v0

v2 whole, which is shorter than its diff:
```python
import jax
import jax.numpy as jnp
from jax import lax
from jax.experimental import pallas as pl
from jax.experimental.pallas import tpu as pltpu
from jax.sharding import PartitionSpec as P

HEAD = 128
HEADS = 16
TOK = 16
LEN = 192
LEN_PAD = 208
HALF = 2048
WIDTH = 4096
FF = 768
EXPERTS = 128
STRIDES = (16, 4, 1)
ORDERS = ((1, 0, 2), (0, 2, 1), (2, 1, 0))
SIZES = (768, 640, 640)
FIRSTS = (0, 768, 1408)
MESH = pl.DeviceIdType.MESH
VMEM_LIMIT = 56 * 2**20
BF = jnp.bfloat16
F32 = jnp.float32


def rows_dot(a, b):
    return lax.dot_general(a, b, (((1,), (1,)), ((), ())), preferred_element_type=F32)


def dot(a, b):
    return jnp.dot(a, b, preferred_element_type=F32)


def iotas(rows, cols):
    shape = (rows, cols)
    return lax.broadcasted_iota(jnp.int32, shape, 0), lax.broadcasted_iota(jnp.int32, shape, 1)


def kernel(
    lengths,
    ids,
    route,
    gain,
    queries,
    new_keys,
    new_values,
    keys_hbm,
    values_hbm,
    gate_hbm,
    up_hbm,
    down_hbm,
    out,
    *scratch,
):
    refs = list(scratch)

    def take(count):
        taken = refs[:count]
        del refs[:count]
        return taken

    gathered, picked, arrived, produced, returned, partial, parts, summed, pieces, resid, meta = (
        take(3) for _ in range(11)
    )
    (keys, values, heads, gate_w, up_w, down_w, normed, gate, up, hidden) = take(10)
    select, combine = take(2)
    (load_sem, weight_sem, meta_sem, g1_sem, g2_sem, ex_sem, back_sem, r1_sem, r2_sem, own_sem) = (
        take(10)
    )

    role = lax.axis_index("role")
    dev = lax.axis_index("dev")
    here = (dev // 16, (dev // 4) % 4, dev % 4)

    def at(axis, value):
        return dev + (value - here[axis]) * STRIDES[axis]

    def along(axis, step):
        return lax.rem(here[axis] + step, 4)

    def send(src, dst, send_sem, recv_sem, target):
        pltpu.make_async_remote_copy(
            src_ref=src,
            dst_ref=dst,
            send_sem=send_sem,
            recv_sem=recv_sem,
            device_id=target,
            device_id_type=MESH,
        ).start()

    def pair(sems, b, k):
        return sems.at[0, b, k], sems.at[1, b, k]

    def keep(src, dst, sems, b, k):
        pltpu.make_async_copy(src, dst, sems.at[1, b, k]).start()

    def settle(ref, sem):
        pltpu.make_async_copy(ref, ref, sem).wait()

    loads = []
    for b in range(2):
        span = pl.ds(b * TOK, TOK)
        for n, (src, dst) in enumerate(((keys_hbm, keys), (values_hbm, values))):
            copy = pltpu.make_async_copy(
                src.at[span, 0], dst.at[span, pl.ds(0, LEN)], load_sem.at[b, n]
            )
            copy.start()
            loads.append(copy)
    weights = [
        pltpu.make_async_copy(src.at[0], dst, weight_sem.at[n])
        for n, (src, dst) in enumerate(((gate_hbm, gate_w), (up_hbm, up_w), (down_hbm, down_w)))
    ]

    barrier = pltpu.get_barrier_semaphore()
    for axis in range(3):
        for step in (1, 2, 3):
            for who in range(2):
                pl.semaphore_signal(
                    barrier, inc=1, device_id=(who, at(axis, along(axis, step))), device_id_type=MESH
                )
    pl.semaphore_signal(barrier, inc=1, device_id=(1 - role, dev), device_id_type=MESH)

    both = 2 * TOK
    row, col = iotas(EXPERTS, both)
    share = route[...] / jnp.sum(route[...], axis=0, keepdims=True)
    named = ids[...]
    hit = jnp.zeros((EXPERTS, both), F32)
    shares = jnp.zeros((EXPERTS, both), F32)
    for k in range(named.shape[0]):
        same = named[k : k + 1, :] == row
        hit = jnp.where(same, 1.0, hit)
        shares = jnp.where(same, share[k : k + 1, :], shares)
    row, col = iotas(both, both)
    before = jnp.where((row // TOK == col // TOK) & (row < col), 1.0, 0.0).astype(BF)
    second = dot(hit.astype(BF), before)
    signed = jnp.where(second > 0.5, -shares, shares).astype(BF)
    signed = rows_dot(jnp.where(row == col, 1.0, 0.0).astype(BF), signed).astype(BF)
    for k, (a1, a2, _) in enumerate(ORDERS):
        meta[k][here[a2], here[a1]] = signed

    scale = HEAD ** (-0.5)
    first_row = lax.broadcasted_iota(jnp.int32, (16, HEAD), 0) == 0
    place = lax.broadcasted_iota(jnp.int32, (HEADS, LEN_PAD), 1)

    def attend(first):
        scores = []
        for n in range(8):
            r = first + n
            own_key = jnp.broadcast_to(new_keys[pl.ds(r, 1), :], (16, HEAD)).astype(F32)
            own_value = jnp.broadcast_to(new_values[pl.ds(r, 1), :], (16, HEAD)).astype(F32)
            keys[r, LEN:LEN_PAD, :] = jnp.where(first_row, own_key, 0.0).astype(BF)
            values[r, LEN:LEN_PAD, :] = jnp.where(first_row, own_value, 0.0).astype(BF)
            live = (place < lengths[r]) | (place == LEN)
            scores.append(jnp.where(live, rows_dot(queries[r], keys[r]) * scale, -jnp.inf))
        scores = jnp.concatenate(scores, axis=0)
        spread = jnp.exp(scores - jnp.max(scores, axis=1, keepdims=True))
        spread = (spread / jnp.sum(spread, axis=1, keepdims=True)).astype(BF)
        for n in range(8):
            r = first + n
            heads[r * HEADS : (r + 1) * HEADS, :] = dot(
                spread[n * HEADS : (n + 1) * HEADS], values[r]
            )

    def attend_batch(b):
        loads[2 * b].wait()
        loads[2 * b + 1].wait()
        for n in range(2):
            attend(b * TOK + n * 8)

    def put(b):
        for k, (a1, a2, _) in enumerate(ORDERS):
            block = gathered[k].at[b, here[a2], here[a1]]
            for h in range(SIZES[k] // HEAD):
                head = FIRSTS[k] // HEAD + h
                block[:, h * HEAD : (h + 1) * HEAD] = heads[
                    pl.ds(b * TOK * HEADS + head, TOK, stride=HEADS), :
                ].astype(BF)
            for step in (2, 1, 3):
                send(block, block, *pair(g1_sem, b, k), (role, at(a1, along(a1, step))))

    def relay(b):
        for k, (a1, a2, _) in enumerate(ORDERS):
            settle(gathered[k].at[b, 0, pl.ds(0, 3)], g1_sem.at[1, b, k])
            block = gathered[k].at[b, here[a2]]
            for step in (2, 1, 3):
                send(block, block, *pair(g2_sem, b, k), (role, at(a2, along(a2, step))))

    def tables(b):
        row, col = iotas(256, EXPERTS)
        tall_row, tall_col = iotas(256, 256)
        for k, (_, _, a3) in enumerate(ORDERS):
            expert = ((row // 32) % 2) * 64 + at(a3, row // 64)
            chosen = jnp.where(expert == col, 1.0, 0.0).astype(BF)
            marks = meta[k][:, :, b * TOK : (b + 1) * TOK, :].reshape(256, EXPERTS)
            wide = rows_dot(chosen, marks)
            wide = jnp.where(tall_row % 2 == 0, wide, -wide)
            mask = ((tall_row % 32) // 2 == tall_col // TOK) & (wide > 0.0)
            select[b, k] = jnp.where(mask, 1.0, 0.0).astype(BF)
            tall = rows_dot(marks, chosen)
            tall = jnp.where(tall_col % 2 == 0, tall, -tall)
            mask = ((tall_col % 32) // 2 == tall_row // TOK) & (tall > 0.0)
            combine[b, k] = jnp.where(mask, tall, 0.0).astype(BF)

    def pick(b):
        for k, (_, _, a3) in enumerate(ORDERS):
            settle(gathered[k].at[b, pl.ds(0, 3)], g2_sem.at[1, b, k])
            rows = dot(select[b, k], gathered[k][b].reshape(256, SIZES[k]))
            picked[k][b] = rows.astype(BF).reshape(8, 32, SIZES[k])
            there = arrived[k].at[b, role, here[a3]]
            for step in (2, 1, 3):
                z = along(a3, step)
                for who in range(2):
                    send(picked[k].at[b, z * 2 + who], there, *pair(ex_sem, b, k), (who, at(a3, z)))
            mine = here[a3] * 2
            send(picked[k].at[b, mine + 1 - role], there, *pair(ex_sem, b, k), (1 - role, dev))
            keep(picked[k].at[b, mine + role], there, ex_sem, b, k)

    def turned(index, k):
        a1, a2, a3 = ORDERS[0]
        place = {a3: index // 32, a2: (index // 8) % 4, a1: (index // 2) % 4}
        a1, a2, a3 = ORDERS[k]
        return place[a3] * 32 + place[a2] * 8 + place[a1] * 2 + index % 2

    def expert_in(b):
        squares = jnp.zeros((128, HEAD), F32)
        row, col = iotas(128, 128)
        for k in range(3):
            settle(arrived[k].at[b], ex_sem.at[1, b, k])
            for c in range(2):
                rows = arrived[k][b, c].reshape(128, SIZES[k])
                if k == 0:
                    rows = rows.astype(F32)
                else:
                    rows = dot(jnp.where(turned(row, k) == col, 1.0, 0.0).astype(BF), rows)
                for t in range(SIZES[k] // HEAD):
                    tile = rows[:, t * HEAD : (t + 1) * HEAD]
                    squares = squares + tile * tile
                begin = c * HALF + FIRSTS[k]
                normed[:, begin : begin + SIZES[k]] = (
                    rows * gain[:, begin : begin + SIZES[k]]
                ).astype(BF)
        if b == 0:
            weights[0].wait()
            weights[1].wait()

        def tile(n, carry):
            cols = pl.ds(pl.multiple_of(n * 256, 256), 256)
            gate[:, cols] = dot(normed[...], gate_w[:, cols])
            up[:, cols] = dot(normed[...], up_w[:, cols])
            return carry

        lax.fori_loop(0, FF // 256, tile, 0)
        factor = lax.rsqrt(jnp.sum(squares, axis=1, keepdims=True) * (1.0 / WIDTH) + 1e-06)
        gated = gate[...] * factor
        hidden[0] = (gated / (1.0 + jnp.exp(-gated)) * (up[...] * factor)).astype(BF)
        for k in (1, 2):
            turn = jnp.where(turned(col, k) == row, 1.0, 0.0).astype(BF)
            hidden[k] = dot(turn, hidden[0]).astype(BF)

    def expert_out(b):
        if b == 0:
            weights[2].wait()
        for k, (_, _, a3) in enumerate(ORDERS):
            for c in range(2):
                begin = c * HALF + FIRSTS[k]
                rows = dot(hidden[k], down_w[:, begin : begin + SIZES[k]])
                produced[k][b, c] = rows.astype(BF).reshape(4, 32, SIZES[k])
            there = returned[k].at[b, here[a3] * 2 + role]
            for step in (2, 1, 3):
                z = along(a3, step)
                for who in range(2):
                    send(produced[k].at[b, who, z], there, *pair(back_sem, b, k), (who, at(a3, z)))
            send(produced[k].at[b, 1 - role, here[a3]], there, *pair(back_sem, b, k), (1 - role, dev))
            keep(produced[k].at[b, role, here[a3]], there, back_sem, b, k)

    def merge(b):
        for k, (_, a2, _) in enumerate(ORDERS):
            settle(returned[k].at[b], back_sem.at[1, b, k])
            rows = dot(combine[b, k], returned[k][b].reshape(256, SIZES[k]))
            partial[k][b] = rows.astype(BF).reshape(4, 64, SIZES[k])
            there = parts[k].at[b, here[a2]]
            for step in (2, 1, 3):
                z = along(a2, step)
                send(partial[k].at[b, z], there, *pair(r1_sem, b, k), (role, at(a2, z)))
            keep(partial[k].at[b, here[a2]], there, r1_sem, b, k)

    def fold(b):
        for k, (a1, _, _) in enumerate(ORDERS):
            settle(parts[k].at[b], r1_sem.at[1, b, k])
            total = parts[k][b, 0].astype(F32)
            for n in range(1, 4):
                total = total + parts[k][b, n].astype(F32)
            summed[k][b] = total.astype(BF).reshape(4, TOK, SIZES[k])
            there = pieces[k].at[role, here[a1]]
            for step in (2, 1, 3):
                z = along(a1, step)
                send(summed[k].at[b, z], there, r2_sem.at[0, b, k], r2_sem.at[1, 0, k], (b, at(a1, z)))

            @pl.when(role == b)
            def _(k=k, a1=a1, there=there):
                keep(summed[k].at[b, here[a1]], there, r2_sem, 0, k)

            @pl.when(role != b)
            def _(k=k, a1=a1, there=there):
                send(
                    summed[k].at[b, here[a1]],
                    there,
                    own_sem.at[0, 1, k],
                    r2_sem.at[1, 0, k],
                    (b, dev),
                )

    pl.semaphore_wait(barrier, 19)
    for k, (a1, a2, _) in enumerate(ORDERS):
        block = meta[k].at[here[a2], here[a1]]
        for step in (2, 1, 3):
            send(block, block, *pair(meta_sem, 0, k), (role, at(a1, along(a1, step))))
    attend_batch(0)
    put(0)
    attend_batch(1)
    put(1)
    for copy in weights:
        copy.start()
    for k, (a1, a2, _) in enumerate(ORDERS):
        settle(meta[k].at[0, pl.ds(0, 3)], meta_sem.at[1, 0, k])
        block = meta[k].at[here[a2]]
        for step in (2, 1, 3):
            send(block, block, *pair(meta_sem, 1, k), (role, at(a2, along(a2, step))))
    relay(0)
    for k, (a1, a2, _) in enumerate(ORDERS):
        send(
            gathered[k].at[1 - role, here[a2], here[a1]],
            resid[k].at[role],
            *pair(own_sem, 0, k),
            (1 - role, dev),
        )
        keep(gathered[k].at[role, here[a2], here[a1]], resid[k].at[role], own_sem, 0, k)
    relay(1)
    for k in range(3):
        settle(meta[k].at[pl.ds(0, 3)], meta_sem.at[1, 1, k])
    tables(0)
    pick(0)
    tables(1)
    pick(1)
    expert_in(0)
    expert_out(0)
    expert_in(1)
    expert_out(1)
    merge(0)
    merge(1)
    fold(0)
    fold(1)

    for k in range(3):
        settle(pieces[k], r2_sem.at[1, 0, k])
        settle(resid[k], own_sem.at[1, 0, k])
        for c in range(2):
            total = resid[k][c].astype(F32)
            for n in range(4):
                total = total + pieces[k][c, n].astype(F32)
            begin = c * HALF + FIRSTS[k]
            out[:, begin : begin + SIZES[k]] = total.astype(BF)

    for k in range(3):
        settle(meta[k].at[0, pl.ds(0, 3)], meta_sem.at[0, 0, k])
        settle(meta[k].at[pl.ds(0, 3)], meta_sem.at[0, 1, k])
        settle(resid[k].at[0], own_sem.at[0, 0, k])
        for b in range(2):
            settle(gathered[k].at[b, 0, pl.ds(0, 3)], g1_sem.at[0, b, k])
            settle(gathered[k].at[b, pl.ds(0, 3)], g2_sem.at[0, b, k])
            settle(picked[k].at[b, pl.ds(0, 7)], ex_sem.at[0, b, k])
            settle(picked[k].at[b, pl.ds(0, 7)], back_sem.at[0, b, k])
            settle(partial[k].at[b, pl.ds(0, 3)], r1_sem.at[0, b, k])
            settle(summed[k].at[b, pl.ds(0, 3)], r2_sem.at[0, b, k])
        settle(resid[k].at[0], own_sem.at[0, 1, k])


def per_device(
    queries,
    keys_cache,
    values_cache,
    new_keys,
    new_values,
    lengths,
    norm_gain,
    expert_ids,
    route_weights,
    gate_weight,
    up_weight,
    down_weight,
):
    def buffers(*lead):
        return [pltpu.VMEM((*lead, size), BF) for size in SIZES]

    vmem = pl.BlockSpec(memory_space=pltpu.VMEM)
    hbm = pl.BlockSpec(memory_space=pl.ANY)
    mixed = pl.pallas_call(
        kernel,
        name="layer",
        out_shape=jax.ShapeDtypeStruct((TOK, WIDTH), BF),
        in_specs=[pl.BlockSpec(memory_space=pltpu.SMEM)] + [vmem] * 6 + [hbm] * 5,
        out_specs=vmem,
        scratch_shapes=[
            *buffers(2, 4, 4, TOK),
            *buffers(2, 8, 32),
            *buffers(2, 2, 4, 32),
            *buffers(2, 2, 4, 32),
            *buffers(2, 8, 32),
            *buffers(2, 4, 64),
            *buffers(2, 4, 64),
            *buffers(2, 4, TOK),
            *buffers(2, 4, TOK),
            *buffers(2, TOK),
            *[pltpu.VMEM((4, 4, 2 * TOK, EXPERTS), BF)] * 3,
            pltpu.VMEM((2 * TOK, LEN_PAD, HEAD), BF),
            pltpu.VMEM((2 * TOK, LEN_PAD, HEAD), BF),
            pltpu.VMEM((2 * TOK * HEADS, HEAD), F32),
            pltpu.VMEM((WIDTH, FF), BF),
            pltpu.VMEM((WIDTH, FF), BF),
            pltpu.VMEM((FF, WIDTH), BF),
            pltpu.VMEM((128, WIDTH), BF),
            pltpu.VMEM((128, FF), F32),
            pltpu.VMEM((128, FF), F32),
            pltpu.VMEM((3, 128, FF), BF),
            pltpu.VMEM((2, 3, 256, 256), BF),
            pltpu.VMEM((2, 3, 256, 256), BF),
            pltpu.SemaphoreType.DMA((2, 2)),
            pltpu.SemaphoreType.DMA((3,)),
            *[pltpu.SemaphoreType.DMA((2, 2, 3))] * 8,
        ],
        compiler_params=pltpu.CompilerParams(
            collective_id=0, has_side_effects=True, vmem_limit_bytes=VMEM_LIMIT
        ),
        cost_estimate=pl.CostEstimate(
            flops=6 * 256 * WIDTH * FF, bytes_accessed=22 * 2**20, transcendentals=0
        ),
    )(
        lengths,
        expert_ids.T,
        route_weights.T,
        norm_gain.reshape(1, WIDTH),
        queries,
        new_keys.reshape(2 * TOK, HEAD),
        new_values.reshape(2 * TOK, HEAD),
        keys_cache,
        values_cache,
        gate_weight,
        up_weight,
        down_weight,
    )
    return mixed.reshape(1, 1, TOK, WIDTH)


def solution(mesh):
    return jax.shard_map(
        per_device,
        mesh=mesh,
        in_specs=(
            P("dev", "role", None),
            P("dev", "role", None, None),
            P("dev", "role", None, None),
            P("dev", "role", None),
            P("dev", "role", None),
            P("dev"),
            P(),
            P("dev", None),
            P("dev", None),
            P(("role", "dev"), None, None),
            P(("role", "dev"), None, None),
            P(("role", "dev"), None, None),
        ),
        out_specs=P("dev", "role", None, None),
        check_vma=False,
    )
```

time: 126 us -> 59.2 us (0.47)
  Pallas kernels: 0 us -> 57.5 us
  blocking collectives: 39.3 us -> 0 us
  waiting for transfers between devices: 28.1 us -> 0 us
  matrix products: 24.4 us -> 0 us
  local copies, waits for them, and re-layouts: 18.7 us -> 1.57 us
  starting transfers between devices: 11.6 us -> 0 us
  other arithmetic: 3.32 us -> 0 us
    pallas_call x0 -> x1, Pallas kernels: none -> 57.5 us  [per_device(): pl.pallas_call(kernel, name='layer', out_shape=jax.ShapeDtypeStruct((TOK,...]
    all_to_all x1 -> x0, blocking collectives: 39.3 us -> none  [per_device(): lax.all_to_all(outgoing, ('role', 'dev'), split_axis=0, concat_axis=0, ti...]
    all_to_all x2 -> x0, waiting for transfers between devices: 28.1 us -> none  [the longest x1 27.6 us: per_device(): lax.all_to_all(produced, ('role', 'dev'), split_axis=0, concat_axis=0, ti...]
    dot_general x7 -> x0, matrix products: 24.4 us -> none  [the longest x1 11.1 us: run_expert(): out = jnp.dot(hidden, down_weight[0], preferred_element_type=jnp.float32)]
    reshape x5 -> x0, local copies, waits for them, and re-layouts: 17.1 us -> none  [the longest x1 4.4 us: run_expert(): return out.astype(jnp.bfloat16).reshape(sources, slots, width)]
    all_to_all x2 -> x0, starting transfers between devices: 11.6 us -> none  [the longest x1 6.85 us: per_device(): lax.all_to_all(produced, ('role', 'dev'), split_axis=0, concat_axis=0, ti...]
    unnamed x11 -> x1, local copies, waits for them, and re-layouts: 0.1 us -> 1.57 us
  transfers between devices with their start and end apart: 2 -> 0, of which waited for: 2 -> 0; matrix products, arithmetic and copies ran while one was open for 1% -> 0% of each run, Pallas kernels for 0% -> 0%
where the time goes in v2:
time: 59.2 us; the launch traced here: 59.1 us
  Pallas kernels  57.5 us (97%)
  local copies, waits for them, and re-layouts  1.57 us (3%)
    pallas_call x1, Pallas kernels, per_device(): pl.pallas_call(kernel, name='layer', out_shape=jax.ShapeDtypeStruct((TOK,...  57.5 us
    unnamed x1, local copies, waits for them, and re-layouts  1.57 us

profile of v2, /device:TPU:1, one launch (start us, length us, event | category | flops | bytes accessed | tf_op | source)
XLA Modules:
  0.0 59.1 jit_solution(8166479680365447019)
XLA Ops:
  0.0 57.5 %layer.1 = bf16[16,4096]{1,0:T(8,128)(2,1)} custom-call(s32[32]{0:T(128)} %lengths.1, s32[8,32]{1,0:T(8,128)} %bitcast.10, f32[8,32]{1,0:T(8,128)} %bitcast.11, f32[1,4096]{1,0:T(1,128)} %bitcast.7, bf16[32,16,128]{2,1,0:T(8,128)(2,1)} %queries.1, bf16[32,128]{1,0:T(8,128)(2,1)} %bitcast.8, bf16[32,128]{1,0:T(8,128)(2,1)} %bitcast.9, ...), custom_call_target="tpu_custom_call" | custom-call | flops 4831838208 | bytes 23068672 | tf_op jit(solution)/shard_map/layer/pallas_call | solution.py:398
  57.5 1.6 %copy.14 = bf16[1,1,16,4096]{3,2,1,0:T(8,128)(2,1)} copy(bf16[1,1,16,4096]{3,2,1,0:T(8,128)(2,1)} %bitcast.6) | data formatting | bytes 262144

commit v3 on v2

v3 whole, which is shorter than its diff:
```python
import jax
import jax.numpy as jnp
from jax import lax
from jax.experimental import pallas as pl
from jax.experimental.pallas import tpu as pltpu
from jax.sharding import PartitionSpec as P

HEAD = 128
HEADS = 16
TOK = 16
LEN = 192
LEN_PAD = 208
HALF = 2048
WIDTH = 4096
FF = 768
EXPERTS = 128
STRIDES = (16, 4, 1)
ORDERS = ((1, 0, 2), (0, 2, 1), (2, 1, 0))
SIZES = (768, 640, 640)
FIRSTS = (0, 768, 1408)
CHUNKS = (((0, 384), (0, 384), (0, 256)), ((384, 384), (384, 256), (256, 384)))
DISPATCH = ((0, 1), (None,))
RETURN = ((None,), (0, 1))
MESH = pl.DeviceIdType.MESH
VMEM_LIMIT = 52 * 2**20
BF = jnp.bfloat16
F32 = jnp.float32


def rows_dot(a, b):
    return lax.dot_general(a, b, (((1,), (1,)), ((), ())), preferred_element_type=F32)


def dot(a, b):
    return jnp.dot(a, b, preferred_element_type=F32)


def iotas(rows, cols):
    shape = (rows, cols)
    return lax.broadcasted_iota(jnp.int32, shape, 0), lax.broadcasted_iota(jnp.int32, shape, 1)


def span(j, k):
    return (0, SIZES[k]) if j is None else CHUNKS[j][k]


def kernel(*refs):
    small_hbm = refs[:7]
    keys_hbm, values_hbm, gate_hbm, up_hbm, down_hbm, out = refs[7:13]
    lengths, ids, route, gain, queries, new_keys, new_values = small = refs[13:20]
    refs = list(refs[20:])

    def take(count):
        taken = refs[:count]
        del refs[:count]
        return taken

    gathered, picked, arrived, produced, returned, partial, parts, summed, pieces, resid, meta = (
        take(3) for _ in range(11)
    )
    (keys, values, heads, gate_w, up_w, down_w, normed, gate, up, hidden, squares) = take(11)
    select, combine = take(2)
    (small_sem, load_sem, weight_sem, meta_sem, g1_sem, g2_sem, ex_sem, back_sem, r1_sem, r2_sem, own_sem) = (
        take(11)
    )

    role = lax.axis_index("role")
    dev = lax.axis_index("dev")
    here = (dev // 16, (dev // 4) % 4, dev % 4)

    def at(axis, value):
        return dev + (value - here[axis]) * STRIDES[axis]

    def along(axis, step):
        return lax.rem(here[axis] + step, 4)

    def send(src, dst, send_sem, recv_sem, target):
        pltpu.make_async_remote_copy(
            src_ref=src,
            dst_ref=dst,
            send_sem=send_sem,
            recv_sem=recv_sem,
            device_id=target,
            device_id_type=MESH,
        ).start()

    def pair(sems, *index):
        return sems.at[0, *index], sems.at[1, *index]

    def keep(src, dst, sems, *index):
        pltpu.make_async_copy(src, dst, sems.at[1, *index]).start()

    def lanes(ref, j, k):
        first, size = span(j, k)
        return ref if j is None else ref.at[..., pl.ds(first, size)]

    def settle(ref, sem):
        pltpu.make_async_copy(ref, ref, sem).wait()

    small_loads = [
        pltpu.make_async_copy(src, dst, small_sem.at[n])
        for n, (src, dst) in enumerate(zip(small_hbm, small))
    ]
    loads = [
        pltpu.make_async_copy(
            src.at[pl.ds(n * 8, 8), 0], dst.at[pl.ds(n * 8, 8), pl.ds(0, LEN)], load_sem.at[n, m]
        )
        for n in range(4)
        for m, (src, dst) in enumerate(((keys_hbm, keys), (values_hbm, values)))
    ]
    for copy in small_loads[:3] + loads[:2] + small_loads[3:] + loads[2:]:
        copy.start()

    def load_weights():
        for n, (src, dst) in enumerate(((gate_hbm, gate_w), (up_hbm, up_w))):
            for j in range(2):
                place = j * HALF
                for c in range(2):
                    for k in range(3):
                        first, size = CHUNKS[j][k]
                        pltpu.make_async_copy(
                            src.at[0, pl.ds(c * HALF + FIRSTS[k] + first, size)],
                            dst.at[pl.ds(place, size)],
                            weight_sem.at[n, j],
                        ).start()
                        place += size
        pltpu.make_async_copy(down_hbm.at[0], down_w, weight_sem.at[2, 0]).start()

    barrier = pltpu.get_barrier_semaphore()
    for axis in range(3):
        for step in (1, 2, 3):
            for who in range(2):
                pl.semaphore_signal(
                    barrier, inc=1, device_id=(who, at(axis, along(axis, step))), device_id_type=MESH
                )
    pl.semaphore_signal(barrier, inc=1, device_id=(1 - role, dev), device_id_type=MESH)

    small_loads[1].wait()
    small_loads[2].wait()
    both = 2 * TOK
    row, col = iotas(EXPERTS, both)
    share = route[...] / jnp.sum(route[...], axis=0, keepdims=True)
    named = ids[...]
    hit = jnp.zeros((EXPERTS, both), F32)
    shares = jnp.zeros((EXPERTS, both), F32)
    for k in range(named.shape[0]):
        same = named[k : k + 1, :] == row
        hit = jnp.where(same, 1.0, hit)
        shares = jnp.where(same, share[k : k + 1, :], shares)
    row, col = iotas(both, both)
    before = jnp.where((row // TOK == col // TOK) & (row < col), 1.0, 0.0).astype(BF)
    second = dot(hit.astype(BF), before)
    signed = jnp.where(second > 0.5, -shares, shares).astype(BF)
    signed = rows_dot(jnp.where(row == col, 1.0, 0.0).astype(BF), signed).astype(BF)
    for k, (a1, a2, _) in enumerate(ORDERS):
        meta[k][here[a2], here[a1]] = signed

    scale = HEAD ** (-0.5)
    first_row = lax.broadcasted_iota(jnp.int32, (16, HEAD), 0) == 0
    place = lax.broadcasted_iota(jnp.int32, (HEADS, LEN_PAD), 1)

    def attend(first):
        scores = []
        for n in range(8):
            r = first + n
            own_key = jnp.broadcast_to(new_keys[pl.ds(r, 1), :], (16, HEAD)).astype(F32)
            own_value = jnp.broadcast_to(new_values[pl.ds(r, 1), :], (16, HEAD)).astype(F32)
            keys[r, LEN:LEN_PAD, :] = jnp.where(first_row, own_key, 0.0).astype(BF)
            values[r, LEN:LEN_PAD, :] = jnp.where(first_row, own_value, 0.0).astype(BF)
            live = (place < lengths[r]) | (place == LEN)
            scores.append(jnp.where(live, rows_dot(queries[r], keys[r]) * scale, -jnp.inf))
        scores = jnp.concatenate(scores, axis=0)
        spread = jnp.exp(scores - jnp.max(scores, axis=1, keepdims=True))
        spread = (spread / jnp.sum(spread, axis=1, keepdims=True)).astype(BF)
        for n in range(8):
            r = first + n
            heads[r * HEADS : (r + 1) * HEADS, :] = dot(
                spread[n * HEADS : (n + 1) * HEADS], values[r]
            )

    def attend_batch(b):
        for n in range(2 * b, 2 * b + 2):
            loads[2 * n].wait()
            loads[2 * n + 1].wait()
            attend(n * 8)

    def put(b, j):
        for k, (a1, a2, _) in enumerate(ORDERS):
            first, size = span(j, k)
            block = gathered[k].at[b, here[a2], here[a1]]
            for h in range(first // HEAD, (first + size) // HEAD):
                head = FIRSTS[k] // HEAD + h
                block[:, h * HEAD : (h + 1) * HEAD] = heads[
                    pl.ds(b * TOK * HEADS + head, TOK, stride=HEADS), :
                ].astype(BF)
            block = lanes(block, j, k)
            for step in (2, 1, 3):
                send(block, block, *pair(g1_sem, b, j or 0, k), (role, at(a1, along(a1, step))))

    def relay(b, j):
        for k, (a1, a2, _) in enumerate(ORDERS):
            settle(lanes(gathered[k].at[b, 0, pl.ds(0, 3)], j, k), g1_sem.at[1, b, j or 0, k])
            block = lanes(gathered[k].at[b, here[a2]], j, k)
            for step in (2, 1, 3):
                send(block, block, *pair(g2_sem, b, j or 0, k), (role, at(a2, along(a2, step))))

    def tables(b):
        row, col = iotas(256, EXPERTS)
        tall_row, tall_col = iotas(256, 256)
        for k, (_, _, a3) in enumerate(ORDERS):
            expert = ((row // 32) % 2) * 64 + at(a3, row // 64)
            chosen = jnp.where(expert == col, 1.0, 0.0).astype(BF)
            marks = meta[k][:, :, b * TOK : (b + 1) * TOK, :].reshape(256, EXPERTS)
            wide = rows_dot(chosen, marks)
            wide = jnp.where(tall_row % 2 == 0, wide, -wide)
            mask = ((tall_row % 32) // 2 == tall_col // TOK) & (wide > 0.0)
            select[b, k] = jnp.where(mask, 1.0, 0.0).astype(BF)
            tall = rows_dot(marks, chosen)
            tall = jnp.where(tall_col % 2 == 0, tall, -tall)
            mask = ((tall_col % 32) // 2 == tall_row // TOK) & (tall > 0.0)
            combine[b, k] = jnp.where(mask, tall, 0.0).astype(BF)

    def pick(b, j):
        for k, (_, _, a3) in enumerate(ORDERS):
            first, size = span(j, k)
            settle(lanes(gathered[k].at[b, pl.ds(0, 3)], j, k), g2_sem.at[1, b, j or 0, k])
            tokens = gathered[k][b, :, :, :, first : first + size].reshape(256, size)
            rows = dot(select[b, k], tokens).astype(BF)
            picked[k][b, :, :, first : first + size] = rows.reshape(8, 32, size)
            there = lanes(arrived[k].at[b, role, here[a3]], j, k)
            sems = pair(ex_sem, b, j or 0, k)
            for step in (2, 1, 3):
                z = along(a3, step)
                for who in range(2):
                    send(lanes(picked[k].at[b, z * 2 + who], j, k), there, *sems, (who, at(a3, z)))
            mine = here[a3] * 2
            send(lanes(picked[k].at[b, mine + 1 - role], j, k), there, *sems, (1 - role, dev))
            keep(lanes(picked[k].at[b, mine + role], j, k), there, ex_sem, b, j or 0, k)

    def turned(index, k):
        a1, a2, a3 = ORDERS[0]
        place = {a3: index // 32, a2: (index // 8) % 4, a1: (index // 2) % 4}
        a1, a2, a3 = ORDERS[k]
        return place[a3] * 32 + place[a2] * 8 + place[a1] * 2 + index % 2

    def expert_in(b, j):
        row, col = iotas(128, 128)
        chunks = (0, 1) if j is None else (j,)
        total = jnp.zeros((128, HEAD), F32) if 0 in chunks else squares[...]
        for k in range(3):
            settle(lanes(arrived[k].at[b], j, k), ex_sem.at[1, b, j or 0, k])
            for part in chunks:
                place = part * HALF + sum(size for _, size in CHUNKS[part][:k])
                for c in range(2):
                    first, size = CHUNKS[part][k]
                    rows = arrived[k][b, c, :, :, first : first + size].reshape(128, size)
                    if k == 0:
                        rows = rows.astype(F32)
                    else:
                        rows = dot(jnp.where(turned(row, k) == col, 1.0, 0.0).astype(BF), rows)
                    for t in range(size // HEAD):
                        tile = rows[:, t * HEAD : (t + 1) * HEAD]
                        total = total + tile * tile
                    begin = c * HALF + FIRSTS[k] + first
                    normed[:, place : place + size] = (rows * gain[:, begin : begin + size]).astype(BF)
                    place += 1024
        squares[...] = total
        if b == 0:
            for part in chunks:
                settle(gate_w.at[pl.ds(part * HALF, HALF)], weight_sem.at[0, part])
                settle(up_w.at[pl.ds(part * HALF, HALF)], weight_sem.at[1, part])
        begin, end = chunks[0] * HALF, (chunks[-1] + 1) * HALF

        def tile(n, carry):
            cols = pl.ds(pl.multiple_of(n * 256, 256), 256)
            for total, weight in ((gate, gate_w), (up, up_w)):
                product = dot(normed[:, begin:end], weight[begin:end, cols])
                total[:, cols] = product if 0 in chunks else total[:, cols] + product
            return carry

        lax.fori_loop(0, FF // 256, tile, 0)

    def expert_mid():
        row, col = iotas(128, 128)
        factor = lax.rsqrt(jnp.sum(squares[...], axis=1, keepdims=True) * (1.0 / WIDTH) + 1e-06)
        gated = gate[...] * factor
        hidden[0] = (gated / (1.0 + jnp.exp(-gated)) * (up[...] * factor)).astype(BF)
        for k in (1, 2):
            turn = jnp.where(turned(col, k) == row, 1.0, 0.0).astype(BF)
            hidden[k] = dot(turn, hidden[0]).astype(BF)

    def expert_out(b, j):
        if b == 0 and j != 1:
            settle(down_w, weight_sem.at[2, 0])
        for k, (_, _, a3) in enumerate(ORDERS):
            first, size = span(j, k)
            for c in range(2):
                begin = c * HALF + FIRSTS[k] + first
                rows = dot(hidden[k], down_w[:, begin : begin + size]).astype(BF)
                produced[k][b, c, :, :, first : first + size] = rows.reshape(4, 32, size)
            there = lanes(returned[k].at[b, here[a3] * 2 + role], j, k)
            sems = pair(back_sem, b, j or 0, k)
            for step in (2, 1, 3):
                z = along(a3, step)
                for who in range(2):
                    send(lanes(produced[k].at[b, who, z], j, k), there, *sems, (who, at(a3, z)))
            mine = produced[k].at[b, :, here[a3]]
            send(lanes(mine.at[1 - role], j, k), there, *sems, (1 - role, dev))
            keep(lanes(mine.at[role], j, k), there, back_sem, b, j or 0, k)

    def merge(b, j):
        for k, (_, a2, _) in enumerate(ORDERS):
            first, size = span(j, k)
            settle(lanes(returned[k].at[b], j, k), back_sem.at[1, b, j or 0, k])
            rows = returned[k][b, :, :, first : first + size].reshape(256, size)
            rows = dot(combine[b, k], rows).astype(BF)
            partial[k][b, :, :, first : first + size] = rows.reshape(4, 64, size)
            there = lanes(parts[k].at[b, here[a2]], j, k)
            for step in (2, 1, 3):
                z = along(a2, step)
                send(
                    lanes(partial[k].at[b, z], j, k),
                    there,
                    *pair(r1_sem, b, j or 0, k),
                    (role, at(a2, z)),
                )
            keep(lanes(partial[k].at[b, here[a2]], j, k), there, r1_sem, b, j or 0, k)

    def fold(b, j):
        for k, (a1, _, _) in enumerate(ORDERS):
            first, size = span(j, k)
            settle(lanes(parts[k].at[b], j, k), r1_sem.at[1, b, j or 0, k])
            total = parts[k][b, 0, :, first : first + size].astype(F32)
            for n in range(1, 4):
                total = total + parts[k][b, n, :, first : first + size].astype(F32)
            summed[k][b, :, :, first : first + size] = total.astype(BF).reshape(4, TOK, size)
            there = lanes(pieces[k].at[role, here[a1]], j, k)
            arrival = r2_sem.at[1, 0, 0, k]
            for step in (2, 1, 3):
                z = along(a1, step)
                send(
                    lanes(summed[k].at[b, z], j, k),
                    there,
                    r2_sem.at[0, b, j or 0, k],
                    arrival,
                    (b, at(a1, z)),
                )
            mine = lanes(summed[k].at[b, here[a1]], j, k)

            @pl.when(role == b)
            def _(mine=mine, there=there, arrival=arrival):
                pltpu.make_async_copy(mine, there, arrival).start()

            @pl.when(role != b)
            def _(mine=mine, there=there, arrival=arrival, k=k):
                send(mine, there, own_sem.at[0, 1, j or 0, k], arrival, (b, dev))

    def left_dispatch():
        for k in range(3):
            settle(meta[k].at[0, pl.ds(0, 3)], meta_sem.at[0, 0, 0, k])
            settle(meta[k].at[pl.ds(0, 3)], meta_sem.at[0, 1, 0, k])
            settle(resid[k].at[0], own_sem.at[0, 0, 0, k])
            for b in range(2):
                for j in DISPATCH[b]:
                    block = lanes(gathered[k].at[b], j, k)
                    settle(block.at[0, pl.ds(0, 3)], g1_sem.at[0, b, j or 0, k])
                    settle(block.at[pl.ds(0, 3)], g2_sem.at[0, b, j or 0, k])
                    settle(lanes(picked[k].at[b, pl.ds(0, 7)], j, k), ex_sem.at[0, b, j or 0, k])

    def left_return(buffers, sems, blocks):
        for k in range(3):
            for b in range(2):
                for j in RETURN[b]:
                    block = lanes(buffers[k].at[b, pl.ds(0, blocks)], j, k)
                    settle(block, sems.at[0, b, j or 0, k])

    pl.semaphore_wait(barrier, 19)
    for k, (a1, a2, _) in enumerate(ORDERS):
        block = meta[k].at[here[a2], here[a1]]
        for step in (2, 1, 3):
            send(block, block, *pair(meta_sem, 0, 0, k), (role, at(a1, along(a1, step))))
    for n in (0, 3, 4, 5, 6):
        small_loads[n].wait()
    attend_batch(0)
    for j in DISPATCH[0]:
        put(0, j)
    attend_batch(1)
    for j in DISPATCH[1]:
        put(1, j)
    load_weights()
    for k, (a1, a2, _) in enumerate(ORDERS):
        settle(meta[k].at[0, pl.ds(0, 3)], meta_sem.at[1, 0, 0, k])
        block = meta[k].at[here[a2]]
        for step in (2, 1, 3):
            send(block, block, *pair(meta_sem, 1, 0, k), (role, at(a2, along(a2, step))))
    for j in DISPATCH[0]:
        relay(0, j)
    for k, (a1, a2, _) in enumerate(ORDERS):
        send(
            gathered[k].at[1 - role, here[a2], here[a1]],
            resid[k].at[role],
            *pair(own_sem, 0, 0, k),
            (1 - role, dev),
        )
        keep(gathered[k].at[role, here[a2], here[a1]], resid[k].at[role], own_sem, 0, 0, k)
    for j in DISPATCH[1]:
        relay(1, j)
    for k in range(3):
        settle(meta[k].at[pl.ds(0, 3)], meta_sem.at[1, 1, 0, k])
    tables(0)
    pick(0, 0)
    pick(0, 1)
    tables(1)
    pick(1, None)
    expert_in(0, 0)
    expert_in(0, 1)
    expert_mid()
    expert_out(0, None)
    expert_in(1, None)
    expert_mid()
    expert_out(1, 0)
    expert_out(1, 1)
    left_dispatch()
    merge(0, None)
    merge(1, 0)
    merge(1, 1)
    left_return(picked, back_sem, 7)
    fold(0, None)
    fold(1, 0)
    fold(1, 1)
    left_return(partial, r1_sem, 3)
    for k in range(3):
        settle(pieces[k], r2_sem.at[1, 0, 0, k])
        settle(resid[k], own_sem.at[1, 0, 0, k])
        for c in range(2):
            total = resid[k][c].astype(F32)
            for n in range(4):
                total = total + pieces[k][c, n].astype(F32)
            begin = c * HALF + FIRSTS[k]
            out[:, begin : begin + SIZES[k]] = total.astype(BF)

    for k in range(3):
        for b in range(2):
            for j in RETURN[b]:
                settle(lanes(summed[k].at[b, pl.ds(0, 3)], j, k), r2_sem.at[0, b, j or 0, k])

                @pl.when(role != b)
                def _(j=j, k=k):
                    settle(lanes(resid[k].at[0], j, k), own_sem.at[0, 1, j or 0, k])


def per_device(
    queries,
    keys_cache,
    values_cache,
    new_keys,
    new_values,
    lengths,
    norm_gain,
    expert_ids,
    route_weights,
    gate_weight,
    up_weight,
    down_weight,
):
    def buffers(*lead):
        return [pltpu.VMEM((*lead, size), BF) for size in SIZES]

    operands = (
        lengths,
        expert_ids.T,
        route_weights.T,
        norm_gain.reshape(1, WIDTH),
        queries,
        new_keys.reshape(2 * TOK, HEAD),
        new_values.reshape(2 * TOK, HEAD),
        keys_cache,
        values_cache,
        gate_weight,
        up_weight,
        down_weight,
    )
    hbm = pl.BlockSpec(memory_space=pltpu.HBM)
    mixed = pl.pallas_call(
        kernel,
        name="layer",
        out_shape=jax.ShapeDtypeStruct((TOK, WIDTH), BF),
        in_specs=[hbm] * 12,
        out_specs=pl.BlockSpec(memory_space=pltpu.VMEM),
        scratch_shapes=[
            pltpu.SMEM((2 * TOK,), jnp.int32),
            pltpu.VMEM((8, 2 * TOK), jnp.int32),
            pltpu.VMEM((8, 2 * TOK), F32),
            pltpu.VMEM((1, WIDTH), F32),
            pltpu.VMEM((2 * TOK, HEADS, HEAD), BF),
            pltpu.VMEM((2 * TOK, HEAD), BF),
            pltpu.VMEM((2 * TOK, HEAD), BF),
            *buffers(2, 4, 4, TOK),
            *buffers(2, 8, 32),
            *buffers(2, 2, 4, 32),
            *buffers(2, 2, 4, 32),
            *buffers(2, 8, 32),
            *buffers(2, 4, 64),
            *buffers(2, 4, 64),
            *buffers(2, 4, TOK),
            *buffers(2, 4, TOK),
            *buffers(2, TOK),
            *[pltpu.VMEM((4, 4, 2 * TOK, EXPERTS), BF)] * 3,
            pltpu.VMEM((2 * TOK, LEN_PAD, HEAD), BF),
            pltpu.VMEM((2 * TOK, LEN_PAD, HEAD), BF),
            pltpu.VMEM((2 * TOK * HEADS, HEAD), F32),
            pltpu.VMEM((WIDTH, FF), BF),
            pltpu.VMEM((WIDTH, FF), BF),
            pltpu.VMEM((FF, WIDTH), BF),
            pltpu.VMEM((128, WIDTH), BF),
            pltpu.VMEM((128, FF), F32),
            pltpu.VMEM((128, FF), F32),
            pltpu.VMEM((3, 128, FF), BF),
            pltpu.VMEM((128, HEAD), F32),
            pltpu.VMEM((2, 3, 256, 256), BF),
            pltpu.VMEM((2, 3, 256, 256), BF),
            pltpu.SemaphoreType.DMA((7,)),
            pltpu.SemaphoreType.DMA((4, 2)),
            pltpu.SemaphoreType.DMA((3, 2)),
            *[pltpu.SemaphoreType.DMA((2, 2, 2, 3))] * 8,
        ],
        compiler_params=pltpu.CompilerParams(
            collective_id=0, has_side_effects=True, vmem_limit_bytes=VMEM_LIMIT
        ),
        cost_estimate=pl.CostEstimate(
            flops=6 * 256 * WIDTH * FF, bytes_accessed=22 * 2**20, transcendentals=0
        ),
    )(*(pltpu.with_memory_space_constraint(operand, pltpu.HBM) for operand in operands))
    return mixed.reshape(1, 1, TOK, WIDTH)


def solution(mesh):
    return jax.shard_map(
        per_device,
        mesh=mesh,
        in_specs=(
            P("dev", "role", None),
            P("dev", "role", None, None),
            P("dev", "role", None, None),
            P("dev", "role", None),
            P("dev", "role", None),
            P("dev"),
            P(),
            P("dev", None),
            P("dev", None),
            P(("role", "dev"), None, None),
            P(("role", "dev"), None, None),
            P(("role", "dev"), None, None),
        ),
        out_specs=P("dev", "role", None, None),
        check_vma=False,
    )
```

time: 59.2 us -> 56.5 us (0.954)
  Pallas kernels: 57.5 us -> 55.8 us
  local copies, waits for them, and re-layouts: 1.57 us -> 0.66 us
    pallas_call x1, Pallas kernels: 57.5 us -> 55.8 us  [per_device(): pl.pallas_call(kernel, name='layer', out_shape=jax.ShapeDtypeStruct((TOK,...]
    unnamed x1, local copies, waits for them, and re-layouts: 1.57 us -> 0.66 us
where the time goes in v3:
time: 56.5 us; the launch traced here: 56.4 us
  Pallas kernels  55.8 us (99%)
  local copies, waits for them, and re-layouts  0.66 us (1%)
    pallas_call x1, Pallas kernels, per_device(): pl.pallas_call(kernel, name='layer', out_shape=jax.ShapeDtypeStruct((TOK,...  55.8 us

profile of v3, /device:TPU:1, one launch (start us, length us, event | category | flops | bytes accessed | tf_op | source)
XLA Modules:
  0.0 56.4 jit_solution(6157631232637885275)
XLA Ops:
  0.0 55.8 %layer.1 = bf16[16,4096]{1,0:T(8,128)(2,1)S(1)} custom-call(s32[32]{0:T(128)} %refs_0_.1, s32[8,32]{1,0:T(8,128)} %bitcast.10, f32[8,32]{1,0:T(8,128)} %bitcast.11, f32[1,4096]{1,0:T(1,128)} %bitcast.7, bf16[32,16,128]{2,1,0:T(8,128)(2,1)} %refs_4_.1, bf16[32,128]{1,0:T(8,128)(2,1)} %bitcast.8, bf16[32,128]{1,0:T(8,128)(2,1)} %bitcast.9, ...), custom_call_target="tpu_custom_call" | custom-call | flops 4831838208 | bytes 23068672 | tf_op jit(solution)/shard_map/layer/pallas_call | solution.py:484
  55.8 0.7 %copy.14 = bf16[1,1,16,4096]{3,2,1,0:T(8,128)(2,1)} copy(bf16[1,1,16,4096]{3,2,1,0:T(8,128)(2,1)S(1)} %bitcast.6) | data formatting | bytes 262144

commit v4 on v3

--- a/solution.py
+++ b/solution.py
@@ -58,6 +58,7 @@
     gathered, picked, arrived, produced, returned, partial, parts, summed, pieces, resid, meta = (
         take(3) for _ in range(11)
     )
+    brief, inbox = take(3), take(3)
     (keys, values, heads, gate_w, up_w, down_w, normed, gate, up, hidden, squares) = take(11)
     select, combine = take(2)
     (small_sem, load_sem, weight_sem, meta_sem, g1_sem, g2_sem, ex_sem, back_sem, r1_sem, r2_sem, own_sem) = (
@@ -108,7 +109,7 @@
         for n in range(4)
         for m, (src, dst) in enumerate(((keys_hbm, keys), (values_hbm, values)))
     ]
-    for copy in small_loads[:3] + loads[:2] + small_loads[3:] + loads[2:]:
+    for copy in small_loads[1:3]:
         copy.start()
 
     def load_weights():
@@ -134,6 +135,9 @@
                     barrier, inc=1, device_id=(who, at(axis, along(axis, step))), device_id_type=MESH
                 )
     pl.semaphore_signal(barrier, inc=1, device_id=(1 - role, dev), device_id_type=MESH)
+
+    for copy in small_loads[:1] + loads[:2] + small_loads[3:] + loads[2:]:
+        copy.start()
 
     small_loads[1].wait()
     small_loads[2].wait()
@@ -205,20 +209,21 @@
                 send(block, block, *pair(g2_sem, b, j or 0, k), (role, at(a2, along(a2, step))))
 
     def tables(b):
-        row, col = iotas(256, EXPERTS)
-        tall_row, tall_col = iotas(256, 256)
-        for k, (_, _, a3) in enumerate(ORDERS):
-            expert = ((row // 32) % 2) * 64 + at(a3, row // 64)
-            chosen = jnp.where(expert == col, 1.0, 0.0).astype(BF)
-            marks = meta[k][:, :, b * TOK : (b + 1) * TOK, :].reshape(256, EXPERTS)
-            wide = rows_dot(chosen, marks)
-            wide = jnp.where(tall_row % 2 == 0, wide, -wide)
-            mask = ((tall_row % 32) // 2 == tall_col // TOK) & (wide > 0.0)
+        row, col = iotas(256, 16)
+        expand = jnp.where(row // 32 == col, 1.0, 0.0).astype(BF)
+        row, col = iotas(128, 256)
+        lane = jnp.where(row == (col % 64) // TOK * 2 * TOK + b * TOK + col % TOK, 1.0, 0.0)
+        row, place = iotas(256, 256)
+        for k in range(3):
+            marks = jnp.zeros((16, 256), F32)
+            for n in range(4):
+                spread = jnp.where(col // 64 == n, lane, 0.0).astype(BF)
+                marks = marks + dot(inbox[k][n], spread)
+            wide = dot(expand, marks.astype(BF))
+            wide = jnp.where(row % 2 == 0, wide, -wide)
+            mask = ((row % 32) // 2 == place // TOK) & (wide > 0.0)
             select[b, k] = jnp.where(mask, 1.0, 0.0).astype(BF)
-            tall = rows_dot(marks, chosen)
-            tall = jnp.where(tall_col % 2 == 0, tall, -tall)
-            mask = ((tall_col % 32) // 2 == tall_row // TOK) & (tall > 0.0)
-            combine[b, k] = jnp.where(mask, tall, 0.0).astype(BF)
+            combine[b, k] = jnp.where(mask, wide, 0.0).T.astype(BF)
 
     def pick(b, j):
         for k, (_, _, a3) in enumerate(ORDERS):
@@ -271,14 +276,14 @@
                 settle(up_w.at[pl.ds(part * HALF, HALF)], weight_sem.at[1, part])
         begin, end = chunks[0] * HALF, (chunks[-1] + 1) * HALF
 
-        def tile(n, carry):
-            cols = pl.ds(pl.multiple_of(n * 256, 256), 256)
+        def tile(n):
+            cols = pl.ds(n * 256, 256)
             for total, weight in ((gate, gate_w), (up, up_w)):
                 product = dot(normed[:, begin:end], weight[begin:end, cols])
                 total[:, cols] = product if 0 in chunks else total[:, cols] + product
-            return carry
-
-        lax.fori_loop(0, FF // 256, tile, 0)
+
+        for n in range(FF // 256):
+            tile(n)
 
     def expert_mid():
         row, col = iotas(128, 128)
@@ -358,7 +363,7 @@
     def left_dispatch():
         for k in range(3):
             settle(meta[k].at[0, pl.ds(0, 3)], meta_sem.at[0, 0, 0, k])
-            settle(meta[k].at[pl.ds(0, 3)], meta_sem.at[0, 1, 0, k])
+            settle(inbox[k].at[pl.ds(0, 3)], meta_sem.at[0, 1, 0, k])
             settle(resid[k].at[0], own_sem.at[0, 0, 0, k])
             for b in range(2):
                 for j in DISPATCH[b]:
@@ -388,11 +393,22 @@
     for j in DISPATCH[1]:
         put(1, j)
     load_weights()
-    for k, (a1, a2, _) in enumerate(ORDERS):
+    row, col = iotas(64, EXPERTS)
+    for k, (a1, a2, a3) in enumerate(ORDERS):
         settle(meta[k].at[0, pl.ds(0, 3)], meta_sem.at[1, 0, 0, k])
-        block = meta[k].at[here[a2]]
+        shift = (row // 16 - here[a2]) * STRIDES[a2] + ((row // 2) % 4 - here[a3]) * STRIDES[a3]
+        wanted = jnp.where((row % 2) * 64 + dev + shift == col, 1.0, 0.0).astype(BF)
+        shares = rows_dot(wanted, meta[k][here[a2]].reshape(128, EXPERTS))
+        brief[k][...] = shares.astype(BF).reshape(4, 16, 128)
+        inbox[k][here[a2]] = brief[k][here[a2]]
         for step in (2, 1, 3):
-            send(block, block, *pair(meta_sem, 1, 0, k), (role, at(a2, along(a2, step))))
+            there = along(a2, step)
+            send(
+                brief[k].at[there],
+                inbox[k].at[here[a2]],
+                *pair(meta_sem, 1, 0, k),
+                (role, at(a2, there)),
+            )
     for j in DISPATCH[0]:
         relay(0, j)
     for k, (a1, a2, _) in enumerate(ORDERS):
@@ -406,7 +422,7 @@
     for j in DISPATCH[1]:
         relay(1, j)
     for k in range(3):
-        settle(meta[k].at[pl.ds(0, 3)], meta_sem.at[1, 1, 0, k])
+        settle(inbox[k].at[pl.ds(0, 3)], meta_sem.at[1, 1, 0, k])
     tables(0)
     pick(0, 0)
     pick(0, 1)
@@ -506,6 +522,7 @@
             *buffers(2, 4, TOK),
             *buffers(2, TOK),
             *[pltpu.VMEM((4, 4, 2 * TOK, EXPERTS), BF)] * 3,
+            *[pltpu.VMEM((4, 16, 128), BF)] * 6,
             pltpu.VMEM((2 * TOK, LEN_PAD, HEAD), BF),
             pltpu.VMEM((2 * TOK, LEN_PAD, HEAD), BF),
             pltpu.VMEM((2 * TOK * HEADS, HEAD), F32),

time: 56.5 us -> 54.9 us (0.972)
  Pallas kernels: 55.8 us -> 54.1 us
    pallas_call x1, Pallas kernels: 55.8 us -> 54.1 us  [per_device(): pl.pallas_call(kernel, name='layer', out_shape=jax.ShapeDtypeStruct((TOK,...]
where the time goes in v4:
time: 54.9 us; the launch traced here: 54.7 us
  Pallas kernels  54.1 us (99%)
  local copies, waits for them, and re-layouts  0.66 us (1%)
    pallas_call x1, Pallas kernels, per_device(): pl.pallas_call(kernel, name='layer', out_shape=jax.ShapeDtypeStruct((TOK,...  54.1 us

profile of v4, /device:TPU:1, one launch (start us, length us, event | category | flops | bytes accessed | tf_op | source)
XLA Modules:
  0.0 54.7 jit_solution(8610305793836602545)
XLA Ops:
  0.0 54.1 %layer.1 = bf16[16,4096]{1,0:T(8,128)(2,1)S(1)} custom-call(s32[32]{0:T(128)} %refs_0_.1, s32[8,32]{1,0:T(8,128)} %bitcast.10, f32[8,32]{1,0:T(8,128)} %bitcast.11, f32[1,4096]{1,0:T(1,128)} %bitcast.7, bf16[32,16,128]{2,1,0:T(8,128)(2,1)} %refs_4_.1, bf16[32,128]{1,0:T(8,128)(2,1)} %bitcast.8, bf16[32,128]{1,0:T(8,128)(2,1)} %bitcast.9, ...), custom_call_target="tpu_custom_call" | custom-call | flops 4831838208 | bytes 23068672 | tf_op jit(solution)/shard_map/layer/pallas_call | solution.py:500
  54.1 0.7 %copy.14 = bf16[1,1,16,4096]{3,2,1,0:T(8,128)(2,1)} copy(bf16[1,1,16,4096]{3,2,1,0:T(8,128)(2,1)S(1)} %bitcast.6) | data formatting | bytes 262144
